TPU v7x, 256 devices: a whole 4x4x8 slice. The times are simulated.
256 devices in a mesh: wide: 16 (over x_hi, z), narrow: 16 (over x_lo, y, core).
Axes of the slice: x: 4 (x_hi: 2, x_lo: 2; x = x_hi * 2 + x_lo), y: 4, z: 8, core: 2. Of those that a mesh axis runs over, the one named last changes fastest.
Arguments:
- pair_act: bfloat16 [768, 768, 128], P('wide', 'narrow'), may hold values from -6 to 6
- residue_mask: int32 [768], replicated, may hold values 0 or 1
- w_proj_start: bfloat16 [128, 512], replicated, may hold values from -0.5 to 0.5
- w_bias_start: bfloat16 [128, 4], replicated, may hold values from -40 to 40
- w_out_start: bfloat16 [128, 128], replicated, may hold values from -0.5 to 0.5
- w_proj_end: bfloat16 [128, 512], replicated, may hold values from -0.5 to 0.5
- w_bias_end: bfloat16 [128, 4], replicated, may hold values from -40 to 40
- w_out_end: bfloat16 [128, 128], replicated, may hold values from -0.5 to 0.5
Outputs:
- update_start: bfloat16 [768, 768, 128], P('wide', 'narrow')
- update_end: bfloat16 [768, 768, 128], P('wide', 'narrow')
All inputs are finite; a program needn't handle non-finite values.
Results may differ from a plain program's by a relative error of at most 0.012.
The roundings to bfloat16 on the way count: a program that leaves them out, or rounds other values in their place, can miss the bound.
Values may be sent and summed in bfloat16 or wider, within the bound.
A program may use at most 64 MiB of HBM per device.

v0:
```python
import jax
import jax.numpy as jnp
from jax import lax
from jax.sharding import Mesh
from jax.sharding import PartitionSpec as P

NARROW = ("narrow_0", "narrow_1", "narrow_2")
norm_eps = 1e-05
masked_score = -1000000000.0


def cut_along(x, dim, count):
    before, after = (x.shape[:dim], x.shape[dim + 1 :])
    return jnp.moveaxis(x.reshape(*before, count, -1, *after), dim, 0)


def in_order(parts, dim):
    parts = jnp.moveaxis(parts, 0, dim)
    shape = parts.shape
    return parts.reshape(*shape[:dim], shape[dim] * shape[dim + 1], *shape[dim + 2 :])


def turned_blocks(parts, axes, order):
    inside = parts.shape[1:]
    out = parts.reshape(*(lax.axis_size(a) for a in axes), *inside)
    for k in order:
        out = lax.all_to_all(out, axes[k], k, k, tiled=True)
    return out.reshape(-1, *inside)


def two_step_exchange(x, groups, order, split_dim, concat_dim):
    count = lax.axis_size(groups[0]) * lax.axis_size(groups[1])
    parts = cut_along(x, split_dim, count)
    return in_order(turned_blocks(parts, groups, order), concat_dim)


def layer_norm(features):
    average = jnp.mean(features, axis=-1, keepdims=True)
    centred = features - average
    spread = jnp.mean(centred * centred, axis=-1, keepdims=True)
    return (centred * lax.rsqrt(spread + norm_eps)).astype(jnp.bfloat16)


def attend(projected, pair_bias, row_ok, key_ok, head_count, head_dim):
    length = projected.shape[1]
    inv_root = head_dim ** (-0.5)

    def one_row(item_pair):
        packed, valid_row = item_pair
        packed = packed.reshape(length, head_count, 4, head_dim)
        queries = packed[:, :, 0]
        keyset = packed[:, :, 1]
        values = packed[:, :, 2]
        gating = packed[:, :, 3]
        scores = (
            jnp.einsum("bhd,khd->hbk", queries, keyset, preferred_element_type=jnp.float32)
            * inv_root
            + pair_bias
        )
        allowed = jnp.logical_and(valid_row, key_ok)
        scores = jnp.where(allowed[None, None, :], scores, masked_score)
        weights = jax.nn.softmax(scores, axis=-1).astype(jnp.bfloat16)
        summed = jnp.einsum("hbk,khd->bhd", weights, values, preferred_element_type=jnp.float32)
        gated = (jax.nn.sigmoid(gating.astype(jnp.float32)) * summed).astype(jnp.bfloat16)
        return gated.reshape(length, head_count * head_dim)

    return lax.map(one_row, (projected, row_ok))


def on_device(
    pair_act,
    residue_mask,
    w_proj_start,
    w_bias_start,
    w_out_start,
    w_proj_end,
    w_bias_end,
    w_out_end,
):
    wide_count = lax.axis_size("wide")
    narrow_count = lax.axis_size(NARROW)
    wide_at = lax.axis_index("wide")
    narrow_at = lax.axis_index(NARROW)
    tile_rows, tile_cols, channels = pair_act.shape
    head_count = w_bias_start.shape[1]
    head_dim = w_out_start.shape[0] // head_count
    residue_ok = residue_mask > 0
    normed = layer_norm(pair_act.astype(jnp.float32))
    groups = narrow_count // head_count
    sub_rows = tile_rows // groups
    proj_tile = jnp.einsum(
        "ijc,chx->hijx",
        normed,
        w_proj_start.reshape(channels, head_count, -1),
        preferred_element_type=jnp.float32,
    ).astype(jnp.bfloat16)
    outgoing = proj_tile.reshape(narrow_count, sub_rows, tile_cols, -1)
    bias_tile = jnp.einsum("ijc,ch->hij", normed, w_bias_start, preferred_element_type=jnp.float32)
    bias_out = jnp.repeat(bias_tile, groups, axis=0)
    incoming = two_step_exchange(outgoing, (("narrow_0", "narrow_1"), "narrow_2"), (1, 0), 0, 2)
    bias_rows = lax.all_to_all(bias_out, NARROW, split_axis=0, concat_axis=2, tiled=True)
    pair_bias = lax.all_gather(bias_rows, "wide", axis=1, tiled=True)
    group_at = narrow_at % groups
    first_row = wide_at * tile_rows + group_at * sub_rows
    row_ok = lax.dynamic_slice_in_dim(residue_ok, first_row, sub_rows)
    gated = attend(incoming[0], pair_bias, row_ok, residue_ok, 1, head_dim)
    returned = lax.all_to_all(
        gated.reshape(sub_rows, -1), NARROW, split_axis=1, concat_axis=0, tiled=True
    )
    head_tile = returned.reshape(head_count, tile_rows, tile_cols, head_dim)
    update_start = jnp.einsum(
        "hijd,hdc->ijc",
        head_tile,
        w_out_start.reshape(head_count, head_dim, channels),
        preferred_element_type=jnp.float32,
    ).astype(jnp.bfloat16)
    updated = pair_act.astype(jnp.float32) + update_start.astype(jnp.float32)
    normed_end = layer_norm(updated)
    groups_wide = wide_count // head_count
    sub_cols = tile_cols // groups_wide
    proj_end_tile = jnp.einsum(
        "ijc,chx->hjix",
        normed_end,
        w_proj_end.reshape(channels, head_count, -1),
        preferred_element_type=jnp.float32,
    ).astype(jnp.bfloat16)
    outgoing_end = proj_end_tile.reshape(wide_count, sub_cols, tile_rows, -1)
    bias_end_tile = jnp.einsum(
        "ijc,ch->hji", normed_end, w_bias_end, preferred_element_type=jnp.float32
    )
    bias_end_out = jnp.repeat(bias_end_tile, groups_wide, axis=0)
    incoming_end = lax.all_to_all(outgoing_end, "wide", split_axis=0, concat_axis=2, tiled=True)
    bias_cols = lax.all_to_all(bias_end_out, "wide", split_axis=0, concat_axis=2, tiled=True)
    pair_bias_end = lax.all_gather(bias_cols, NARROW, axis=1, tiled=True)
    group_wide = wide_at % groups_wide
    first_col = narrow_at * tile_cols + group_wide * sub_cols
    col_ok = lax.dynamic_slice_in_dim(residue_ok, first_col, sub_cols)
    gated_end = attend(incoming_end[0], pair_bias_end, col_ok, residue_ok, 1, head_dim)
    returned_end = lax.all_to_all(
        gated_end.reshape(sub_cols, -1), "wide", split_axis=1, concat_axis=0, tiled=True
    )
    head_tile_end = returned_end.reshape(head_count, tile_cols, tile_rows, head_dim)
    update_end = jnp.einsum(
        "hjid,hdc->ijc",
        head_tile_end,
        w_out_end.reshape(head_count, head_dim, channels),
        preferred_element_type=jnp.float32,
    ).astype(jnp.bfloat16)
    return (update_start, update_end)


def solution(mesh):
    split = Mesh(
        mesh.devices.reshape(mesh.shape["wide"], 2, 4, 2),
        ("wide", "narrow_0", "narrow_1", "narrow_2"),
    )
    placed = (P("wide", NARROW, None), P(), P(), P(), P(), P(), P(), P())
    return jax.shard_map(
        on_device,
        mesh=split,
        in_specs=placed,
        out_specs=(P("wide", NARROW, None), P("wide", NARROW, None)),
        check_vma=False,
    )
```

profile of v0, /device:TPU:40, one launch (start us, length us, event | category | flops | bytes accessed | tf_op | source)
XLA Modules:
  0.0 379.8 jit_solution(18101503657099255865)
XLA Ops:
  7.2 1.5 convert_reduce_fusion
  8.7 1.8 fusion.21
  10.5 1.9 convolution_bitcast_fusion.3
  12.9 10.5 %all_to_all.95 = f32[16,1,2304]{2,1,0:T(1,128)S(1)} all-to-all(f32[16,1,2304]{2,1,0:T(1,128)S(1)} %reshape.255), channel_id=1, replica_groups=mesh['wide'=16,'narrow_0'=2,'narrow_1'=4,'narrow_2'=2] {'narrow_0','narr..., dimensions={0} | all-to-all | bytes 294912 | tf_op jit(solution)/shard_map/all_to_all | solution.py:101
  23.9 1.0 reduce.8
  25.3 1.0 all_to_all.86
  26.4 1.1 convert_bitcast_fusion.1
  28.3 5.6 %all_to_all.96 = bf16[8,2,1,12,48,128]{5,4,3,0,2,1:T(8,128)(2,1)S(1)} all-to-all(bf16[8,2,1,12,48,128]{5,4,3,0,2,1:T(8,128)(2,1)S(1)} %copy.76), channel_id=1, replica_groups=mesh['wide'=16,'narrow_0'=2,'narrow_1'=4,'narrow_2'=2] {'narrow_2'}, dimensions={1} | all-to-all | bytes 4718592 | tf_op jit(solution)/shard_map/all_to_all | solution.py:27
  33.9 1.8 copy.77
  35.7 5.8 %all-to-all-start.1 = ((bf16[8,2,1,12,48,128]{5,4,3,1,2,0:T(8,128)(2,1)}), bf16[8,2,1,12,48,128]{5,4,3,1,2,0:T(8,128)(2,1)S(1)}, u32[]{:S(2)}, u32[]{:S(2)}) async-start(bf16[8,2,1,12,48,128]{5,4,3,1,2,0:T(8,128)(2,1)} %copy.77), calls=%async_computation.1 | async-start | bytes 4718592 | tf_op jit(solution)/shard_map/all_to_all | solution.py:27
  41.6 28.6 %all-to-all-done.1 = bf16[8,2,1,12,48,128]{5,4,3,1,2,0:T(8,128)(2,1)S(1)} async-done(((bf16[8,2,1,12,48,128]{5,4,3,1,2,0:T(8,128)(2,1)}), bf16[8,2,1,12,48,128]{5,4,3,1,2,0:T(8,128)(2,1)S(1)}, u32[]{:S(2)}, u32[]{:S(2)}) %all-to-all-start.1) | async-done | bytes 2359328 | tf_op jit(solution)/shard_map/all_to_all | solution.py:27
  70.2 2.0 copy.78
  72.2 43.2 %all-gather.3.cloned.1.call-done = f32[1,768,768]{2,0,1:T(1,128)} async-done(((f32[1,48,768]{2,0,1:T(1,128)}), f32[1,768,768]{2,0,1:T(1,128)}) %all-gather.3.cloned.1.call-update) | async-done | bytes 2359312 | tf_op jit(solution)/shard_map/all_gather | solution.py:102
  115.4 5.5 %copy.83 = f32[1,768,768]{1,2,0:T(8,128)S(1)} copy(f32[1,768,768]{2,0,1:T(1,128)} %all-gather.3.cloned.1.call-done) | data formatting | bytes 4718592 | tf_op jit(solution)/shard_map/while | solution.py:67
  121.8 52.3 %while.20 = (s32[]{:T(128)}, bf16[12,768,32]{1,2,0:T(8,128)(2,1)}, bf16[12,768,128]{2,1,0:T(8,128)(2,1)}, pred[12]{0:T(512)(128)(4,1)S(1)}, pred[768]{0:T(1024)(...) while((s32[]{:T(128)}, bf16[12,768,32]{1,2,0:T(8,128)(2,1)}, bf16[12,768,128]{2,1,0:T(8,128)(2,1)}, ...), condition=%wide.region_5.6_spmd, body=%wide.region_2.5_spmd.sunk | while | flops 80952576 | bytes 10489944 | solution.py:67
  125.0 1.1 fusion.50
  129.3 1.1 fusion.50
  133.7 1.1 fusion.50
  138.1 1.1 fusion.50
  142.4 1.1 fusion.50
  146.8 1.1 fusion.50
  151.1 1.1 fusion.50
  155.5 1.1 fusion.50
  159.9 1.1 fusion.50
  164.2 1.1 fusion.50
  168.6 1.1 fusion.50
  172.9 1.1 fusion.50
  174.1 2.0 copy.84
  176.1 3.0 all_to_all.73
  179.2 1.4 copy.85
  180.6 15.9 %all_to_all.97 = bf16[12,16,1536]{2,0,1:T(8,128)(2,1)} all-to-all(bf16[12,16,1536]{2,0,1:T(8,128)(2,1)S(1)} %copy.85), channel_id=1, replica_groups=mesh['wide'=16,'narrow_0'=2,'narrow_1'=4,'narrow_2'=2] {'narrow_0','narr..., dimensions={1} | all-to-all | bytes 1179648 | tf_op jit(solution)/shard_map/all_to_all | solution.py:107
  196.5 3.0 reshape.234
  199.5 1.4 fusion.24
  201.7 1.0 convolution_bitcast_fusion.2
  202.9 1.0 reshape.257
  203.9 6.7 %all-to-all-start.5 = ((f32[16,1,2304]{2,1,0:T(1,128)}), f32[16,1,2304]{2,1,0:T(1,128)S(1)}, u32[]{:S(2)}, u32[]{:S(2)}) async-start(f32[16,1,2304]{2,1,0:T(1,128)} %reshape.257), calls=%async_computation.5 | async-start | bytes 294912 | tf_op jit(solution)/shard_map/all_to_all | solution.py:133
  210.6 1.9 convert_bitcast_fusion
  212.5 2.9 copy.88
  215.5 5.7 %all-to-all-done.5 = f32[16,1,2304]{2,1,0:T(1,128)S(1)} async-done(((f32[16,1,2304]{2,1,0:T(1,128)}), f32[16,1,2304]{2,1,0:T(1,128)S(1)}, u32[]{:S(2)}, u32[]{:S(2)}) %all-to-all-start.5) | async-done | bytes 147488 | tf_op jit(solution)/shard_map/all_to_all | solution.py:133
  221.2 4.0 %all-to-all-start.4 = ((bf16[16,12,48,128]{3,2,1,0:T(8,128)(2,1)}), bf16[16,12,48,128]{3,2,1,0:T(8,128)(2,1)S(1)}, u32[]{:S(2)}, u32[]{:S(2)}) async-start(bf16[16,12,48,128]{3,2,1,0:T(8,128)(2,1)} %bitcast.42), calls=%async_computation.4 | async-start | bytes 4718592 | tf_op jit(solution)/shard_map/all_to_all | solution.py:132
  225.5 1.0 reduce.9
  226.8 1.0 all_to_all.87
  227.9 52.0 %all-to-all-done.4 = bf16[16,12,48,128]{3,2,1,0:T(8,128)(2,1)S(1)} async-done(((bf16[16,12,48,128]{3,2,1,0:T(8,128)(2,1)}), bf16[16,12,48,128]{3,2,1,0:T(8,128)(2,1)S(1)}, u32[]{:S(2)}, u32[]{:S(2)}) %all-to-all-start.4) | async-done | bytes 2359328 | tf_op jit(solution)/shard_map/all_to_all | solution.py:132
  279.9 2.0 copy.89
  281.9 5.5 %copy.94 = f32[1,768,768]{1,2,0:T(8,128)S(1)} copy(f32[1,768,768]{2,0,1:T(1,128)} %all-gather.5.cloned.1.call-done) | data formatting | bytes 4718592 | tf_op jit(solution)/shard_map/while | solution.py:67
  287.4 46.0 %while.21 = (s32[]{:T(128)}, bf16[12,768,32]{1,2,0:T(8,128)(2,1)S(1)}, bf16[12,768,128]{2,1,0:T(8,128)(2,1)}, pred[12]{0:T(512)(128)(4,1)S(1)}, pred[768]{0:T(10...) while((s32[]{:T(128)}, bf16[12,768,32]{1,2,0:T(8,128)(2,1)S(1)}, ...), condition=%wide.region_11.12_spmd, body=%wide.region_8.11_spmd.sunk | while | flops 80952576 | bytes 10489436 | solution.py:67
  287.4 0.9 constant_dynamic-slice_fusion.5
  291.3 0.9 constant_dynamic-slice_fusion.5
  295.1 0.9 constant_dynamic-slice_fusion.5
  298.9 0.9 constant_dynamic-slice_fusion.5
  302.8 0.9 constant_dynamic-slice_fusion.5
  306.6 0.9 constant_dynamic-slice_fusion.5
  310.4 0.9 constant_dynamic-slice_fusion.5
  314.3 0.9 constant_dynamic-slice_fusion.5
  318.1 0.9 constant_dynamic-slice_fusion.5
  322.0 0.9 constant_dynamic-slice_fusion.5
  325.8 0.9 constant_dynamic-slice_fusion.5
  329.6 0.9 constant_dynamic-slice_fusion.5
  333.5 1.1 copy.95
  334.6 2.3 all_to_all.83
  337.3 32.0 %all_to_all.98 = bf16[12,16,1536]{2,0,1:T(8,128)(2,1)S(1)} all-to-all(bf16[12,16,1536]{2,0,1:T(8,128)(2,1)S(1)} %copy.96), channel_id=1, replica_groups=mesh['wide'=16,'narrow_0'=2,'narrow_1'=4,'narrow_2'=2] {'wide'}, dimensions={1} | all-to-all | bytes 1179648 | tf_op jit(solution)/shard_map/all_to_all | solution.py:139
  369.3 1.6 reshape.239
  370.9 1.1 fusion.20
  372.0 1.0 copy.98
  (187 shorter events, 77.9 us)
Async XLA Ops:
  7.2 19.2 %copy-start = (bf16[128,512]{1,0:T(8,128)(2,1)S(1)}, bf16[128,512]{1,0:T(8,128)(2,1)}, u32[]{:S(2)}) copy-start(bf16[128,512]{1,0:T(8,128)(2,1)} %param.14) | copy-start | bytes 393220
  7.2 108.2 %all-gather.3.cloned.1.call-start = ((), (), s32[]{:S(2)}) async-start(), calls=%async_computation.7 | async-start | bytes 2506752 | tf_op jit(solution)/shard_map/all_gather | solution.py:102
  10.5 15.9 %copy-start.1 = (bf16[48,48,128]{2,1,0:T(8,128)(2,1)S(1)}, bf16[48,48,128]{2,1,0:T(8,128)(2,1)}, u32[]{:S(2)}) copy-start(bf16[48,48,128]{2,1,0:T(8,128)(2,1)} %param.12) | copy-start | bytes 1769476
  35.7 5.8 %copy-start.6 = (s32[768]{0:T(1024)S(1)}, s32[768]{0:T(1024)}, u32[]{:S(2)}) copy-start(s32[768]{0:T(1024)} %param.13) | copy-start | bytes 9220
  35.7 34.5 %all-to-all-start.1 = ((bf16[8,2,1,12,48,128]{5,4,3,1,2,0:T(8,128)(2,1)}), bf16[8,2,1,12,48,128]{5,4,3,1,2,0:T(8,128)(2,1)S(1)}, u32[]{:S(2)}, u32[]{:S(2)}) async-start(bf16[8,2,1,12,48,128]{5,4,3,1,2,0:T(8,128)(2,1)} %copy.77), calls=%async_computation.1 | async-start | bytes 4718592 | tf_op jit(solution)/shard_map/all_to_all | solution.py:27
  180.6 18.9 %copy-start.4 = (bf16[128,128]{1,0:T(8,128)(2,1)S(1)}, bf16[128,128]{1,0:T(8,128)(2,1)}, u32[]{:S(2)}) copy-start(bf16[128,128]{1,0:T(8,128)(2,1)} %param.16) | copy-start | bytes 98308
  199.4 2.3 copy-start.7
  200.9 0.8 copy-start.2
  200.9 9.7 %copy-start.3 = (bf16[128,512]{1,0:T(8,128)(2,1)S(1)}, bf16[128,512]{1,0:T(8,128)(2,1)}, u32[]{:S(2)}) copy-start(bf16[128,512]{1,0:T(8,128)(2,1)} %param.17) | copy-start | bytes 393220
  203.9 17.3 %all-to-all-start.5 = ((f32[16,1,2304]{2,1,0:T(1,128)}), f32[16,1,2304]{2,1,0:T(1,128)S(1)}, u32[]{:S(2)}, u32[]{:S(2)}) async-start(f32[16,1,2304]{2,1,0:T(1,128)} %reshape.257), calls=%async_computation.5 | async-start | bytes 294912 | tf_op jit(solution)/shard_map/all_to_all | solution.py:133
  221.2 58.7 %all-to-all-start.4 = ((bf16[16,12,48,128]{3,2,1,0:T(8,128)(2,1)}), bf16[16,12,48,128]{3,2,1,0:T(8,128)(2,1)S(1)}, u32[]{:S(2)}, u32[]{:S(2)}) async-start(bf16[16,12,48,128]{3,2,1,0:T(8,128)(2,1)} %bitcast.42), calls=%async_computation.4 | async-start | bytes 4718592 | tf_op jit(solution)/shard_map/all_to_all | solution.py:132
  225.2 56.7 %all-gather.5.cloned.1.call-start = ((), (), s32[]{:S(2)}) async-start(), calls=%async_computation.8 | async-start | bytes 2506752 | tf_op jit(solution)/shard_map/all_gather | solution.py:134
  337.3 33.6 %copy-start.5 = (bf16[128,128]{1,0:T(8,128)(2,1)S(1)}, bf16[128,128]{1,0:T(8,128)(2,1)}, u32[]{:S(2)}) copy-start(bf16[128,128]{1,0:T(8,128)(2,1)} %param.19) | copy-start | bytes 98308
Sparse Core Ops, SparseCore 0:
  26.5 88.9 all-gather.2
  228.5 46.1 all-gather.4
where the time goes:
time: 382 us; the launch traced here: 380 us
  waiting for transfers between devices  130 us (34%)
  local copies, waits for them, and re-layouts  82.4 us (22%)
  blocking collectives  64 us (17%)
  matrix products  42.6 us (11%)
  other arithmetic  29.4 us (8%)
  starting transfers between devices  16.8 us (4%)
  between operations  14.4 us (4%)
    all_to_all x1, waiting for transfers between devices, on_device(): lax.all_to_all(outgoing_end, 'wide', split_axis=0, concat_axis=2, tiled=T...  52 us
    all_gather x1, waiting for transfers between devices, on_device(): pair_bias = lax.all_gather(bias_rows, 'wide', axis=1, tiled=True)  43.2 us
    dynamic_slice x72, local copies, waits for them, and re-layouts, attend(): return lax.map(one_row, (projected, row_ok))  40.2 us
    all_to_all x1, blocking collectives, on_device(): lax.all_to_all(gated_end.reshape(sub_cols, -1), 'wide', split_axis=1, con...  32 us
    all_to_all x1, waiting for transfers between devices, turned_blocks(): out = lax.all_to_all(out, axes[k], k, k, tiled=True)  28.6 us
    dot_general x24, matrix products, one_row(): jnp.einsum('hbk,khd->bhd', weights, values, preferred_element_type=jnp.fl...  19.8 us
    all_to_all x1, blocking collectives, on_device(): lax.all_to_all(gated.reshape(sub_rows, -1), NARROW, split_axis=1, concat_...  15.9 us
    and x24, other arithmetic, one_row(): allowed = jnp.logical_and(valid_row, key_ok)  14.6 us
  transfers between devices with their start and end apart: 5, of which 4 were waited for; matrix products, arithmetic and copies ran while one was open for 4% of the time, Pallas kernels for 0%

commit v1 on v0

--- a/solution.py
+++ b/solution.py
@@ -99,7 +99,9 @@
     bias_out = jnp.repeat(bias_tile, groups, axis=0)
     incoming = two_step_exchange(outgoing, (("narrow_0", "narrow_1"), "narrow_2"), (1, 0), 0, 2)
     bias_rows = lax.all_to_all(bias_out, NARROW, split_axis=0, concat_axis=2, tiled=True)
-    pair_bias = lax.all_gather(bias_rows, "wide", axis=1, tiled=True)
+    pair_bias = jnp.concatenate(
+        lax.all_to_all(jnp.stack([bias_rows] * lax.axis_size("wide")), "wide", 0, 0), axis=1
+    )
     group_at = narrow_at % groups
     first_row = wide_at * tile_rows + group_at * sub_rows
     row_ok = lax.dynamic_slice_in_dim(residue_ok, first_row, sub_rows)

time: 382 us -> 410 us (1.073)
  starting transfers between devices: 16.8 us -> 39.3 us
  blocking collectives: 64 us -> 48.1 us
  matrix products: 42.6 us -> 50 us
  waiting for transfers between devices: 130 us -> 137 us
  local copies, waits for them, and re-layouts: 82.4 us -> 87.8 us
    all_to_all x0 -> x2, waiting for transfers between devices: none -> 55.5 us  [the longest x1 52.5 us: on_device(): lax.all_to_all(jnp.stack([bias_rows] * lax.axis_size('wide')), 'wide', 0, 0)]
    all_gather x1 -> x0, waiting for transfers between devices: 43.2 us -> none  [on_device(): pair_bias = lax.all_gather(bias_rows, 'wide', axis=1, tiled=True)]
    all_to_all x0 -> x2, starting transfers between devices: none -> 16.7 us  [the longest x1 10.9 us: on_device(): lax.all_to_all(jnp.stack([bias_rows] * lax.axis_size('wide')), 'wide', 0, 0)]
    all_to_all x2 -> x0, blocking collectives: 16.1 us -> none  [the longest x1 10.5 us: on_device(): lax.all_to_all(bias_out, NARROW, split_axis=0, concat_axis=2, tiled=True)]
    dot_general x24, matrix products: 19.8 us -> 27.3 us  [one_row(): jnp.einsum('hbk,khd->bhd', weights, values, preferred_element_type=jnp.fl...]
    all_to_all x1 -> x2, waiting for transfers between devices: 28.6 us -> 23.6 us  [turned_blocks(): out = lax.all_to_all(out, axes[k], k, k, tiled=True)]
    all_to_all x1 -> x2, starting transfers between devices: 5.82 us -> 9.63 us  [turned_blocks(): out = lax.all_to_all(out, axes[k], k, k, tiled=True)]
  transfers between devices with their start and end apart: 5 -> 7, of which waited for: 4 -> 6; matrix products, arithmetic and copies ran while one was open for 4% -> 5% of each run, Pallas kernels for 0% -> 0%
where the time goes in v1:
time: 410 us; the launch traced here: 408 us
  waiting for transfers between devices  137 us (33%)
  local copies, waits for them, and re-layouts  87.8 us (21%)
  matrix products  50 us (12%)
  blocking collectives  48.1 us (12%)
  starting transfers between devices  39.3 us (10%)
  other arithmetic  30.5 us (7%)
  between operations  14.4 us (4%)
    all_to_all x1, waiting for transfers between devices, on_device(): lax.all_to_all(jnp.stack([bias_rows] * lax.axis_size('wide')), 'wide', 0, 0)  52.5 us
    all_to_all x1, waiting for transfers between devices, on_device(): lax.all_to_all(outgoing_end, 'wide', split_axis=0, concat_axis=2, tiled=T...  52.1 us
    dynamic_slice x72, local copies, waits for them, and re-layouts, attend(): return lax.map(one_row, (projected, row_ok))  40.5 us
    all_to_all x1, blocking collectives, on_device(): lax.all_to_all(gated_end.reshape(sub_cols, -1), 'wide', split_axis=1, con...  32 us
    dot_general x24, matrix products, one_row(): jnp.einsum('hbk,khd->bhd', weights, values, preferred_element_type=jnp.fl...  27.3 us
    all_to_all x2, waiting for transfers between devices, turned_blocks(): out = lax.all_to_all(out, axes[k], k, k, tiled=True)  23.6 us
    all_to_all x1, blocking collectives, on_device(): lax.all_to_all(gated.reshape(sub_rows, -1), NARROW, split_axis=1, concat_...  16.1 us
    and x24, other arithmetic, one_row(): allowed = jnp.logical_and(valid_row, key_ok)  15.1 us
  transfers between devices with their start and end apart: 7, of which 6 were waited for; matrix products, arithmetic and copies ran while one was open for 5% of the time, Pallas kernels for 0%

profile of v1, /device:TPU:40, one launch (start us, length us, event | category | flops | bytes accessed | tf_op | source)
XLA Modules:
  0.0 407.6 jit_solution(3901342508315159450)
XLA Ops:
  7.2 1.5 convert_reduce_fusion
  8.7 1.8 fusion.21
  10.5 1.9 convert_bitcast_fusion.1
  12.8 1.8 copy.100
  14.6 3.9 all-to-all-start
  19.6 1.0 reshape.264
  21.6 5.9 %all-to-all-start.2 = ((f32[16,1,2304]{2,1,0:T(1,128)}), f32[16,1,2304]{2,1,0:T(1,128)S(1)}, u32[]{:S(2)}, u32[]{:S(2)}) async-start(f32[16,1,2304]{2,1,0:T(1,128)} %reshape.264), calls=%async_computation.2 | async-start | bytes 294912 | tf_op jit(solution)/shard_map/all_to_all | solution.py:101
  27.4 1.8 copy.101
  29.3 3.0 all-to-all-done.2
  32.3 5.7 %all-to-all-start.1 = ((bf16[8,2,1,12,48,128]{5,4,3,1,2,0:T(8,128)(2,1)}), bf16[8,2,1,12,48,128]{5,4,3,1,2,0:T(8,128)(2,1)S(1)}, u32[]{:S(2)}, u32[]{:S(2)}) async-start(bf16[8,2,1,12,48,128]{5,4,3,1,2,0:T(8,128)(2,1)} %copy.101), calls=%async_computation.1 | async-start | bytes 4718592 | tf_op jit(solution)/shard_map/all_to_all | solution.py:27
  38.5 1.6 reduce.8
  40.1 1.1 reshape.265
  42.1 1.2 stack.4
  43.2 22.7 %all-to-all-done.1 = bf16[8,2,1,12,48,128]{5,4,3,1,2,0:T(8,128)(2,1)S(1)} async-done(((bf16[8,2,1,12,48,128]{5,4,3,1,2,0:T(8,128)(2,1)}), bf16[8,2,1,12,48,128]{5,4,3,1,2,0:T(8,128)(2,1)S(1)}, u32[]{:S(2)}, u32[]{:S(2)}) %all-to-all-start.1) | async-done | bytes 2359328 | tf_op jit(solution)/shard_map/all_to_all | solution.py:27
  65.9 1.7 stack.5
  67.6 10.9 %all-to-all-start.3 = ((f32[16,1,48,768]{3,2,1,0:T(8,128)}), f32[16,1,48,768]{3,2,1,0:T(8,128)}, u32[]{:S(2)}, u32[]{:S(2)}) async-start(f32[16,1,48,768]{3,2,1,0:T(8,128)} %stack.5), calls=%async_computation.3 | async-start | bytes 4718592 | tf_op jit(solution)/shard_map/all_to_all | solution.py:103
  78.6 2.0 copy.102
  80.6 52.5 %all-to-all-done.3 = f32[16,1,48,768]{3,2,1,0:T(8,128)} async-done(((f32[16,1,48,768]{3,2,1,0:T(8,128)}), f32[16,1,48,768]{3,2,1,0:T(8,128)}, u32[]{:S(2)}, u32[]{:S(2)}) %all-to-all-start.3) | async-done | bytes 2359328 | tf_op jit(solution)/shard_map/all_to_all | solution.py:103
  133.0 2.0 copy.106
  135.9 53.3 %while.20 = (s32[]{:T(128)}, bf16[12,768,32]{1,2,0:T(8,128)(2,1)}, bf16[12,768,128]{2,1,0:T(8,128)(2,1)}, pred[12]{0:T(512)(128)(4,1)S(1)}, pred[768]{0:T(1024)(...) while((s32[]{:T(128)}, bf16[12,768,32]{1,2,0:T(8,128)(2,1)}, bf16[12,768,128]{2,1,0:T(8,128)(2,1)}, ...), condition=%wide.region_5.6_spmd, body=%wide.region_2.5_spmd.sunk | while | flops 80952576 | bytes 10489944 | solution.py:67
  139.3 1.1 fusion.50
  143.7 1.1 fusion.50
  148.1 1.1 fusion.50
  152.6 1.1 fusion.50
  157.0 1.1 fusion.50
  161.5 1.1 fusion.50
  165.9 1.1 fusion.50
  170.3 1.1 fusion.50
  174.8 1.1 fusion.50
  179.2 1.1 fusion.50
  183.7 1.1 fusion.50
  188.1 1.1 fusion.50
  189.2 2.0 copy.107
  191.3 3.0 all_to_all.74
  194.3 1.4 copy.108
  195.8 16.1 %all_to_all.96 = bf16[12,16,1536]{2,0,1:T(8,128)(2,1)} all-to-all(bf16[12,16,1536]{2,0,1:T(8,128)(2,1)S(1)} %copy.108), channel_id=1, replica_groups=mesh['wide'=16,'narrow_0'=2,'narrow_1'=4,'narrow_2'=2] {'narrow_0','narr..., dimensions={1} | all-to-all | bytes 1179648 | tf_op jit(solution)/shard_map/all_to_all | solution.py:109
  211.8 3.0 reshape.243
  214.8 1.4 fusion.24
  219.3 8.7 %all-to-all-start.6 = ((f32[16,1,2304]{2,1,0:T(1,128)}), f32[16,1,2304]{2,1,0:T(1,128)S(1)}, u32[]{:S(2)}, u32[]{:S(2)}) async-start(f32[16,1,2304]{2,1,0:T(1,128)} %reshape.266), calls=%async_computation.6 | async-start | bytes 294912 | tf_op jit(solution)/shard_map/all_to_all | solution.py:135
  227.9 1.9 convert_bitcast_fusion
  229.8 2.9 copy.111
  232.8 5.7 %all-to-all-done.6 = f32[16,1,2304]{2,1,0:T(1,128)S(1)} async-done(((f32[16,1,2304]{2,1,0:T(1,128)}), f32[16,1,2304]{2,1,0:T(1,128)S(1)}, u32[]{:S(2)}, u32[]{:S(2)}) %all-to-all-start.6) | async-done | bytes 147488 | tf_op jit(solution)/shard_map/all_to_all | solution.py:135
  238.5 4.0 all-to-all-start.5
  245.1 52.1 %all-to-all-done.5 = bf16[16,12,48,128]{3,2,1,0:T(8,128)(2,1)S(1)} async-done(((bf16[16,12,48,128]{3,2,1,0:T(8,128)(2,1)}), bf16[16,12,48,128]{3,2,1,0:T(8,128)(2,1)S(1)}, u32[]{:S(2)}, u32[]{:S(2)}) %all-to-all-start.5) | async-done | bytes 2359328 | tf_op jit(solution)/shard_map/all_to_all | solution.py:134
  297.2 2.0 copy.112
  299.2 5.5 %copy.117 = f32[1,768,768]{1,2,0:T(8,128)S(1)} copy(f32[1,768,768]{2,0,1:T(1,128)} %all-gather.2.cloned.1.call-done) | data formatting | bytes 4718592 | tf_op jit(solution)/shard_map/while | solution.py:67
  305.6 53.3 %while.21 = (s32[]{:T(128)}, bf16[12,768,32]{1,2,0:T(8,128)(2,1)}, bf16[12,768,128]{2,1,0:T(8,128)(2,1)}, pred[12]{0:T(512)(128)(4,1)S(1)}, pred[768]{0:T(1024)(...) while((s32[]{:T(128)}, bf16[12,768,32]{1,2,0:T(8,128)(2,1)}, bf16[12,768,128]{2,1,0:T(8,128)(2,1)}, ...), condition=%wide.region_11.12_spmd, body=%wide.region_8.11_spmd.sunk | while | flops 80952576 | bytes 10489944 | solution.py:67
  308.9 1.1 fusion.53
  313.3 1.1 fusion.53
  317.8 1.1 fusion.53
  322.2 1.1 fusion.53
  326.6 1.1 fusion.53
  331.1 1.1 fusion.53
  335.5 1.1 fusion.53
  340.0 1.1 fusion.53
  344.4 1.1 fusion.53
  348.9 1.1 fusion.53
  353.3 1.1 fusion.53
  357.8 1.1 fusion.53
  358.9 2.0 copy.118
  361.0 2.3 all_to_all.84
  363.6 32.0 %all_to_all.97 = bf16[12,16,1536]{2,0,1:T(8,128)(2,1)} all-to-all(bf16[12,16,1536]{2,0,1:T(8,128)(2,1)S(1)} %copy.119), channel_id=1, replica_groups=mesh['wide'=16,'narrow_0'=2,'narrow_1'=4,'narrow_2'=2] {'wide'}, dimensions={1} | all-to-all | bytes 1179648 | tf_op jit(solution)/shard_map/all_to_all | solution.py:141
  395.7 3.0 reshape.248
  398.7 1.1 fusion.20
  (191 shorter events, 91.3 us)
Async XLA Ops:
  7.2 3.3 copy-start
  14.6 4.0 copy-start.1
  14.6 4.0 copy-start.7
  14.6 7.0 %all-to-all-start = ((bf16[8,2,1,12,48,128]{5,4,3,0,2,1:T(8,128)(2,1)}), bf16[8,2,1,12,48,128]{5,4,3,0,2,1:T(8,128)(2,1)S(1)}, u32[]{:S(2)}, u32[]{:S(2)}) async-start(bf16[8,2,1,12,48,128]{5,4,3,0,2,1:T(8,128)(2,1)} %copy.100), calls=%async_computation | async-start | bytes 4718592 | tf_op jit(solution)/shard_map/all_to_all | solution.py:27
  21.6 10.7 %all-to-all-start.2 = ((f32[16,1,2304]{2,1,0:T(1,128)}), f32[16,1,2304]{2,1,0:T(1,128)S(1)}, u32[]{:S(2)}, u32[]{:S(2)}) async-start(f32[16,1,2304]{2,1,0:T(1,128)} %reshape.264), calls=%async_computation.2 | async-start | bytes 294912 | tf_op jit(solution)/shard_map/all_to_all | solution.py:101
  32.3 33.6 %all-to-all-start.1 = ((bf16[8,2,1,12,48,128]{5,4,3,1,2,0:T(8,128)(2,1)}), bf16[8,2,1,12,48,128]{5,4,3,1,2,0:T(8,128)(2,1)S(1)}, u32[]{:S(2)}, u32[]{:S(2)}) async-start(bf16[8,2,1,12,48,128]{5,4,3,1,2,0:T(8,128)(2,1)} %copy.101), calls=%async_computation.1 | async-start | bytes 4718592 | tf_op jit(solution)/shard_map/all_to_all | solution.py:27
  67.6 10.9 %copy-start.6 = (s32[768]{0:T(1024)S(1)}, s32[768]{0:T(1024)}, u32[]{:S(2)}) copy-start(s32[768]{0:T(1024)} %param.13) | copy-start | bytes 9220
  67.6 65.4 %all-to-all-start.3 = ((f32[16,1,48,768]{3,2,1,0:T(8,128)}), f32[16,1,48,768]{3,2,1,0:T(8,128)}, u32[]{:S(2)}, u32[]{:S(2)}) async-start(f32[16,1,48,768]{3,2,1,0:T(8,128)} %stack.5), calls=%async_computation.3 | async-start | bytes 4718592 | tf_op jit(solution)/shard_map/all_to_all | solution.py:103
  195.7 19.1 %copy-start.4 = (bf16[128,128]{1,0:T(8,128)(2,1)S(1)}, bf16[128,128]{1,0:T(8,128)(2,1)}, u32[]{:S(2)}) copy-start(bf16[128,128]{1,0:T(8,128)(2,1)} %param.16) | copy-start | bytes 98308
  214.8 2.3 copy-start.8
  216.2 0.8 copy-start.2
  216.3 11.7 %copy-start.3 = (bf16[128,512]{1,0:T(8,128)(2,1)S(1)}, bf16[128,512]{1,0:T(8,128)(2,1)}, u32[]{:S(2)}) copy-start(bf16[128,512]{1,0:T(8,128)(2,1)} %param.17) | copy-start | bytes 393220
  219.3 19.2 %all-to-all-start.6 = ((f32[16,1,2304]{2,1,0:T(1,128)}), f32[16,1,2304]{2,1,0:T(1,128)S(1)}, u32[]{:S(2)}, u32[]{:S(2)}) async-start(f32[16,1,2304]{2,1,0:T(1,128)} %reshape.266), calls=%async_computation.6 | async-start | bytes 294912 | tf_op jit(solution)/shard_map/all_to_all | solution.py:135
  238.5 58.7 %all-to-all-start.5 = ((bf16[16,12,48,128]{3,2,1,0:T(8,128)(2,1)}), bf16[16,12,48,128]{3,2,1,0:T(8,128)(2,1)S(1)}, u32[]{:S(2)}, u32[]{:S(2)}) async-start(bf16[16,12,48,128]{3,2,1,0:T(8,128)(2,1)} %bitcast.43), calls=%async_computation.5 | async-start | bytes 4718592 | tf_op jit(solution)/shard_map/all_to_all | solution.py:134
  242.5 56.7 %all-gather.2.cloned.1.call-start = ((), (), s32[]{:S(2)}) async-start(), calls=%async_computation.8 | async-start | bytes 2506752 | tf_op jit(solution)/shard_map/all_gather | solution.py:136
  363.6 35.0 %copy-start.5 = (bf16[128,128]{1,0:T(8,128)(2,1)S(1)}, bf16[128,128]{1,0:T(8,128)(2,1)}, u32[]{:S(2)}) copy-start(bf16[128,128]{1,0:T(8,128)(2,1)} %param.19) | copy-start | bytes 98308
Sparse Core Ops, SparseCore 0:
  245.8 46.1 all-gather.1
